TPU v7x, 256 devices: a whole 4x4x8 slice. The times are simulated.
256 devices in a mesh: sx: 16 (over z, y_lo), sy: 16 (over y_hi, x, core).
Axes of the slice: x: 4, y: 4 (y_hi: 2, y_lo: 2; y = y_hi * 2 + y_lo), z: 8, core: 2. Of those that a mesh axis runs over, the one named last changes fastest.
Arguments:
- loads: bfloat16 [16, 16, 1024, 128], P('sx', 'sy'), may hold values from -6 to 6
- flex: float32 [16, 16, 1024, 1024], P('sx', 'sy'), may hold values from -1 to 9, as said below
- schur: bfloat16 [16, 16, 1024, 1024], P('sx', 'sy'), may hold values from -1 to 9, as said below
- couple: float32 [16, 16, 4, 1024], P('sx', 'sy'), may hold values from -3 to 3
- corner_perm: int32 [225], replicated, may hold values from 0 to 224, each once
- coarse_inverse: float32 [225, 225], replicated, may hold values from -1 to 4, as said below
Outputs:
- multipliers: float32 [16, 16, 2, 256, 128], P('sx', 'sy')
- residual: float32 [16, 16, 2, 256, 128], P('sx', 'sy')
Inputs may be any that keep to these rules, and one draw needn't show every extreme that they name: `flex`: each subdomain's matrix is symmetric positive definite. `schur`: each subdomain's matrix is symmetric positive definite. `coarse_inverse`: symmetric positive definite.
All inputs are finite; a program needn't handle non-finite values.
Results may differ from a plain program's by a relative error of at most 0.009.
Values sent between devices are 32-bit elements; how exact they have to be, the bound alone decides.
A program may use at most 64 MiB of HBM per device.

v0:
```python
import jax
import jax.numpy as jnp
from jax import lax
from jax.sharding import PartitionSpec as P

ITERS = 4


def passed_along(x, axis, by):
    size = lax.axis_size(axis)
    pairs = [(i, i + by) for i in range(size) if 0 <= i + by < size]
    return lax.ppermute(x, axis, pairs)


def corner_numbers(row_pos, col_pos, rows_sx, cols_sy, corner_perm):
    ncoarse = corner_perm.shape[0]
    corner_k = jnp.arange(4, dtype=jnp.int32)
    grid_row = jnp.asarray(row_pos, jnp.int32)[..., None] + corner_k // 2
    grid_col = jnp.asarray(col_pos, jnp.int32)[..., None] + corner_k % 2
    inside = (
        (grid_row >= 1) & (grid_row <= rows_sx - 1) & (grid_col >= 1) & (grid_col <= cols_sy - 1)
    )
    structural = (grid_row - 1) * (cols_sy - 1) + grid_col - 1
    matches = structural[..., None] == jnp.arange(ncoarse, dtype=jnp.int32)
    looked = jnp.sum(jnp.where(matches, corner_perm, 0), -1)
    return jnp.where(inside, looked, -1)


def per_device(loads, flex, schur, couple, corner_perm, coarse_inverse):
    highest = lax.Precision.HIGHEST
    edge_len = flex.shape[-1] // 4
    ncoarse = coarse_inverse.shape[0]
    rows_sx = lax.axis_size("sx")
    cols_sy = lax.axis_size("sy")
    row_index = lax.axis_index("sx")
    col_index = lax.axis_index("sy")
    flex_local = flex[0, 0]
    schur_local = schur[0, 0]
    couple_local = couple[0, 0]
    coarse_range = jnp.arange(ncoarse, dtype=jnp.int32)
    own_ids = corner_numbers(row_index, col_index, rows_sx, cols_sy, corner_perm)
    own_table = (coarse_range[:, None] == own_ids[None, :]).astype(jnp.float32)
    coarse_rows = jnp.dot(own_table.T, coarse_inverse, precision=highest)
    keep_vertical = (row_index < rows_sx - 1).astype(jnp.float32)
    keep_horizontal = (col_index < cols_sy - 1).astype(jnp.float32)

    def correction(partial_value):
        summed = lax.psum(jnp.dot(own_table, partial_value, precision=highest), ("sx", "sy"))
        return jnp.dot(coarse_rows, summed, precision=highest)

    def operator_local(vec_f32):
        partial_value = jnp.dot(couple_local, vec_f32, precision=highest)
        coarse_part = correction(partial_value)
        local_part = jnp.dot(flex_local, vec_f32, precision=highest)
        return local_part + jnp.dot(couple_local.T, coarse_part, precision=highest)

    def spread(dual_vec):
        vertical = dual_vec[0]
        horizontal = dual_vec[1]
        above = passed_along(vertical, "sx", 1)
        beside = passed_along(horizontal, "sy", 1)
        return jnp.concatenate([-above, vertical, -beside, horizontal], 0)

    def from_local(local_vec):
        upper = local_vec[:edge_len]
        lower = local_vec[edge_len : 2 * edge_len]
        west = local_vec[2 * edge_len : 3 * edge_len]
        east = local_vec[3 * edge_len :]
        below = passed_along(upper, "sx", -1)
        right = passed_along(west, "sy", -1)
        return jnp.stack([(lower - below) * keep_vertical, (east - right) * keep_horizontal], 0)

    def precondition(dual_vec):
        halved = (0.5 * spread(dual_vec)).astype(jnp.bfloat16)
        return 0.5 * from_local(jnp.dot(schur_local, halved, preferred_element_type=jnp.float32))

    def local_inner(first, second):
        return jnp.sum(first * second, axis=(0, 1))

    loads_local = loads[0, 0]
    gap = from_local(operator_local(loads_local.astype(jnp.float32)))
    multipliers = jnp.zeros_like(gap)
    residual = gap

    def residual_product(resid, pre_vec):
        return lax.psum(local_inner(resid, pre_vec), ("sx", "sy"))

    pre_vec = precondition(residual)
    direction = pre_vec
    rz_now = residual_product(residual, pre_vec)
    for step_index in range(ITERS):
        image = from_local(operator_local(spread(direction)))
        step_size = rz_now / lax.psum(local_inner(direction, image), ("sx", "sy"))
        multipliers = multipliers + step_size * direction
        residual = residual - step_size * image
        if step_index < ITERS - 1:
            pre_vec = precondition(residual)
            rz_next = residual_product(residual, pre_vec)
            direction = pre_vec + rz_next / rz_now * direction
            rz_now = rz_next
    return (multipliers[None, None], residual[None, None])


def solution(mesh):
    placed = (
        P("sx", "sy", None, None),
        P("sx", "sy", None, None),
        P("sx", "sy", None, None),
        P("sx", "sy", None, None),
        P(),
        P(),
    )
    return jax.shard_map(
        per_device,
        mesh=mesh,
        in_specs=placed,
        out_specs=(P("sx", "sy", None, None, None), P("sx", "sy", None, None, None)),
        check_vma=False,
    )
```

profile of v0, /device:TPU:1, one launch (start us, length us, event | category | flops | bytes accessed | tf_op | source)
XLA Modules:
  0.0 2031.4 jit_solution(998768432437401806)
XLA Ops:
  11.6 247.0 %all-reduce.7.cloned.1.call-done = f32[225,128]{1,0:T(8,128)} async-done(((f32[225,128]{1,0:T(8,128)}), f32[225,128]{1,0:T(8,128)}) %all-reduce.7.cloned.1.call-update) | async-done | bytes 115216 | tf_op jit(solution)/shard_map/psum | solution.py:48
  261.5 4.2 fusion.54
  267.0 4.4 collective-permute-done
  271.4 4.9 collective-permute-start.2
  276.3 4.0 collective-permute-start.1
  280.3 2.0 collective-permute-start.3
  286.4 6.6 collective-permute-done.4
  293.7 2.3 collective-permute-start.5
  296.0 3.9 collective-permute-done.5
  300.7 3.9 collective-permute-start.6
  304.6 2.1 collective-permute-start.7
  310.6 249.2 %all-reduce.9.cloned.1.call-done = f32[225,128]{1,0:T(8,128)} async-done(((f32[225,128]{1,0:T(8,128)}), f32[225,128]{1,0:T(8,128)}) %all-reduce.9.cloned.1.call-update) | async-done | bytes 115216 | tf_op jit(solution)/shard_map/psum | solution.py:48
  561.9 5.3 fusion.51
  568.5 3.7 collective-permute-start.9
  572.9 3.0 collective-permute-done.9
  576.7 78.4 %all-reduce = (f32[128]{0:T(128)S(1)}, f32[128]{0:T(128)S(1)}) all-reduce(f32[128]{0:T(128)S(1)} %get-tuple-element.3, f32[128]{0:T(128)S(1)} %get-tuple-element.2), channel_id=1, replica_groups=mesh['sx'=16,'sy'=16] {'sx','sy'}, use_global_device_ids=true, to_apply=%region_3.4 | all-reduce | flops 256 | bytes 2048 | tf_op jit(solution)/shard_map/psum | solution.py:86
  655.8 3.1 collective-permute-start.10
  666.7 4.7 collective-permute-done.12
  672.7 84.2 %psum.95 = f32[128]{0:T(128)S(1)} all-reduce(f32[128]{0:T(128)S(1)} %multiply_reduce_fusion.4), channel_id=1, replica_groups=mesh['sx'=16,'sy'=16] {'sx','sy'}, use_global_device_ids=true, to_apply=%region_8.9 | all-reduce | flops 128 | bytes 1024 | tf_op jit(solution)/shard_map/psum | solution.py:86
  756.9 2.2 collective-permute-start.14
  759.1 2.1 collective-permute-start.15
  765.8 243.7 %all-reduce.11.cloned.1.call-done = f32[225,128]{1,0:T(8,128)} async-done(((f32[225,128]{1,0:T(8,128)}), f32[225,128]{1,0:T(8,128)}) %all-reduce.11.cloned.1.call-update) | async-done | bytes 115216 | tf_op jit(solution)/shard_map/psum | solution.py:48
  1011.6 5.3 fusion.48
  1018.2 3.7 collective-permute-start.17
  1022.6 3.0 collective-permute-done.17
  1026.4 78.4 %psum.97 = f32[128]{0:T(128)S(1)} all-reduce(f32[128]{0:T(128)S(1)} %multiply_reduce_fusion.3), channel_id=1, replica_groups=mesh['sx'=16,'sy'=16] {'sx','sy'}, use_global_device_ids=true, to_apply=%region_11.12 | all-reduce | flops 128 | bytes 1024 | tf_op jit(solution)/shard_map/psum | solution.py:93
  1106.2 3.1 collective-permute-start.18
  1117.2 4.7 collective-permute-done.20
  1124.6 83.9 %psum.98 = f32[128]{0:T(128)} all-reduce(f32[128]{0:T(128)} %multiply_reduce_fusion.2), channel_id=1, replica_groups=mesh['sx'=16,'sy'=16] {'sx','sy'}, use_global_device_ids=true, to_apply=%region_13.14 | all-reduce | flops 128 | bytes 1024 | tf_op jit(solution)/shard_map/psum | solution.py:86
  1210.5 2.4 collective-permute-start.22
  1212.8 1.9 collective-permute-start.23
  1219.6 243.6 %all-reduce.13.cloned.1.call-done = f32[225,128]{1,0:T(8,128)} async-done(((f32[225,128]{1,0:T(8,128)}), f32[225,128]{1,0:T(8,128)}) %all-reduce.13.cloned.1.call-update) | async-done | bytes 115216 | tf_op jit(solution)/shard_map/psum | solution.py:48
  1465.3 5.4 fusion.45
  1472.0 3.7 collective-permute-start.25
  1476.4 3.0 collective-permute-done.25
  1481.5 78.4 %psum.100 = f32[128]{0:T(128)} all-reduce(f32[128]{0:T(128)} %multiply_reduce_fusion.1), channel_id=1, replica_groups=mesh['sx'=16,'sy'=16] {'sx','sy'}, use_global_device_ids=true, to_apply=%region_16.17 | all-reduce | flops 128 | bytes 1024 | tf_op jit(solution)/shard_map/psum | solution.py:93
  1561.7 3.3 collective-permute-start.26
  1570.9 6.6 collective-permute-done.28
  1580.1 5.5 collective-permute-done.29
  1587.6 81.2 %psum.101 = f32[128]{0:T(128)S(1)} all-reduce(f32[128]{0:T(128)} %multiply_reduce_fusion), channel_id=1, replica_groups=mesh['sx'=16,'sy'=16] {'sx','sy'}, use_global_device_ids=true, to_apply=%region_18.19 | all-reduce | flops 128 | bytes 1024 | tf_op jit(solution)/shard_map/psum | solution.py:86
  1670.5 2.7 collective-permute-start.30
  1680.4 243.6 %all-reduce.15.cloned.1.call-done = f32[225,128]{1,0:T(8,128)} async-done(((f32[225,128]{1,0:T(8,128)}), f32[225,128]{1,0:T(8,128)}) %all-reduce.15.cloned.1.call-update) | async-done | bytes 115216 | tf_op jit(solution)/shard_map/psum | solution.py:48
  1926.1 5.4 fusion.42
  1932.9 3.7 collective-permute-start.33
  1937.3 3.0 collective-permute-done.33
  1941.6 78.4 %psum.103 = f32[128]{0:T(128)S(1)} all-reduce(f32[128]{0:T(128)} %fusion.71), channel_id=1, replica_groups=mesh['sx'=16,'sy'=16] {'sx','sy'}, use_global_device_ids=true, to_apply=%region_21.22 | all-reduce | flops 128 | bytes 1024 | tf_op jit(solution)/shard_map/psum | solution.py:93
  2020.7 2.1 fusion.74
  2022.9 2.0 fusion.77
  (236 shorter events, 94.0 us)
Async XLA Ops:
  7.2 277.2 %copy-start = (bf16[1,1,1024,1024]{3,2,1,0:T(8,128)(2,1)S(1)}, bf16[1,1,1024,1024]{3,2,1,0:T(8,128)(2,1)}, u32[]{:S(2)}) copy-start(bf16[1,1,1024,1024]{3,2,1,0:T(8,128)(2,1)} %param.8) | copy-start | bytes 6291460
  7.2 251.4 %all-reduce.7.cloned.1.call-start = ((), (), s32[]{:S(2)}) async-start(), calls=%async_computation | async-start | bytes 237568 | tf_op jit(solution)/shard_map/psum | solution.py:48
  8.3 253.2 %copy-start.33 = (s32[4]{0:T(128)}, s32[4]{0:T(128)S(1)}, u32[]{:S(2)}) copy-start(s32[4]{0:T(128)S(1)} %and_select_fusion) | copy-start | bytes 52
  10.4 549.4 %all-reduce.9.cloned.1.call-start = ((), (), s32[]{:S(2)}) async-start(), calls=%async_computation.1 | async-start | bytes 237568 | tf_op jit(solution)/shard_map/psum | solution.py:48
  11.6 255.4 %copy-start.23 = (f32[4,225]{1,0:T(4,128)}, f32[4,225]{1,0:T(4,128)S(1)}, u32[]{:S(2)}) copy-start(f32[4,225]{1,0:T(4,128)S(1)} %fusion.109) | copy-start | bytes 10804
  265.7 5.7 collective-permute-start
  271.4 8.9 collective-permute-start.2
  276.3 7.2 collective-permute-start.1
  280.3 4.0 collective-permute-start.3
  285.1 7.9 collective-permute-start.4
  293.7 6.3 collective-permute-start.5
  300.7 259.1 %copy-start.17 = (f32[256,128]{1,0:T(8,128)}, f32[256,128]{1,0:T(8,128)S(1)}, u32[]{:S(2)}) copy-start(f32[256,128]{1,0:T(8,128)S(1)} %get-tuple-element.81) | copy-start | bytes 393220
  300.7 6.0 collective-permute-start.6
  304.6 4.0 collective-permute-start.7
  310.5 698.9 %all-reduce.11.cloned.1.call-start = ((), (), s32[]{:S(2)}) async-start(), calls=%async_computation.2 | async-start | bytes 237568 | tf_op jit(solution)/shard_map/psum | solution.py:48
  567.2 5.7 collective-permute-start.8
  568.5 7.4 collective-permute-start.9
  655.8 5.3 collective-permute-start.10
  658.9 3.9 collective-permute-start.11
  663.5 7.9 collective-permute-start.12
  664.8 7.0 collective-permute-start.13
  756.9 4.3 collective-permute-start.14
  759.1 4.0 collective-permute-start.15
  765.7 697.5 %all-reduce.13.cloned.1.call-start = ((), (), s32[]{:S(2)}) async-start(), calls=%async_computation.3 | async-start | bytes 237568 | tf_op jit(solution)/shard_map/psum | solution.py:48
  1016.9 5.7 collective-permute-start.16
  1018.2 7.4 collective-permute-start.17
  1106.2 5.3 collective-permute-start.18
  1109.3 3.9 collective-permute-start.19
  1113.9 7.9 collective-permute-start.20
  1115.2 7.0 collective-permute-start.21
  1210.5 4.6 collective-permute-start.22
  1212.8 3.9 collective-permute-start.23
  1219.3 704.7 %all-reduce.15.cloned.1.call-start = ((), (), s32[]{:S(2)}) async-start(), calls=%async_computation.4 | async-start | bytes 237568 | tf_op jit(solution)/shard_map/psum | solution.py:48
  1470.7 5.7 collective-permute-start.24
  1472.0 7.4 collective-permute-start.25
  1561.7 5.6 collective-permute-start.26
  1565.0 3.9 collective-permute-start.27
  1569.6 7.9 collective-permute-start.28
  1578.2 7.4 collective-permute-start.29
  1670.5 4.8 collective-permute-start.30
  1673.2 3.9 collective-permute-start.31
  1675.4 249.7 %copy-start.14 = (f32[256,128]{1,0:T(8,128)}, f32[256,128]{1,0:T(8,128)S(1)}, u32[]{:S(2)}) copy-start(f32[256,128]{1,0:T(8,128)S(1)} %neg.62) | copy-start | bytes 393220
  1678.8 262.2 %copy-start.4 = (f32[1,256,128]{2,1,0:T(8,128)S(1)}, f32[1,256,128]{2,1,0:T(8,128)}, u32[]{:S(2)}) copy-start(f32[1,256,128]{2,1,0:T(8,128)} %copy-done.3) | copy-start | bytes 393220
  1678.8 262.2 %copy-start.10 = (f32[1,256,128]{2,1,0:T(8,128)S(1)}, f32[1,256,128]{2,1,0:T(8,128)}, u32[]{:S(2)}) copy-start(f32[1,256,128]{2,1,0:T(8,128)} %copy-done.9) | copy-start | bytes 393220
  1926.1 96.8 %copy-start.12 = (f32[1,1,1,256,128]{4,3,2,1,0:T(8,128)S(1)}, f32[1,1,1,256,128]{4,3,2,1,0:T(8,128)}, u32[]{:S(2)}) copy-start(f32[1,1,1,256,128]{4,3,2,1,0:T(8,128)} %get-tuple-element.20) | copy-start | bytes 393220
  1926.1 96.8 %copy-start.27 = (f32[128]{0:T(128)S(1)}, f32[128]{0:T(128)}, u32[]{:S(2)}) copy-start(f32[128]{0:T(128)} %copy-done.24) | copy-start | bytes 1540
  1931.6 5.7 collective-permute-start.32
  1932.9 7.4 collective-permute-start.33
  (38 other events, 802.8 us)
Sparse Core Ops, SparseCore 0:
  14.1 244.4 all-reduce.6
  310.7 249.0 all-reduce.8
  765.9 243.5 all-reduce.10
  1219.4 243.7 all-reduce.12
  1680.5 243.3 all-reduce.14
where the time goes:
time: 2030 us
  waiting for transfers between devices  1290 us (64%)
  blocking collectives  563 us (28%)
  starting transfers between devices  80.4 us (4%)
  matrix products  52.4 us (3%)
  other arithmetic  23.9 us (1%)
    psum x5, waiting for transfers between devices, correction(): lax.psum(jnp.dot(own_table, partial_value, precision=highest), ('sx', 'sy'))  1230 us
    psum x4, blocking collectives, residual_product(): return lax.psum(local_inner(resid, pre_vec), ('sx', 'sy'))  328 us
    psum x3, blocking collectives, per_device(): step_size = rz_now / lax.psum(local_inner(direction, image), ('sx', 'sy'))  235 us
    ppermute x34, starting transfers between devices, passed_along(): return lax.ppermute(x, axis, pairs)  80 us
    ppermute x34, waiting for transfers between devices, passed_along(): return lax.ppermute(x, axis, pairs)  66.9 us
  transfers between devices with their start and end apart: 39, of which 36 were waited for; matrix products, arithmetic and copies ran while one was open for 0% of the time, Pallas kernels for 0%

commit v1 on v0

v1 whole, which is shorter than its diff:
```python
import functools

import jax
import jax.numpy as jnp
from jax import lax
from jax.experimental import pallas as pl
from jax.experimental.pallas import tpu as pltpu
from jax.sharding import PartitionSpec as P

ITERS = 4
MESH = pl.DeviceIdType.MESH
F32 = jnp.float32
BF16 = jnp.bfloat16
OPPOSITE = (1, 0, 3, 2)
NEAR = ((-1, 0), (1, 0), (0, -1), (0, 1))


def dot(a, b):
    return jnp.dot(a, b, preferred_element_type=F32)


def halves(x):
    high = x.astype(BF16)
    return high, (x - high.astype(F32)).astype(BF16)


def dot3(a_high, a_low, b_high, b_low):
    return dot(a_high, b_high) + (dot(a_high, b_low) + dot(a_low, b_high))


def colsum(x):
    return jnp.sum(x, axis=0, keepdims=True)


def iota(shape, dim):
    return lax.broadcasted_iota(jnp.int32, shape, dim)


def kernel(
    nx, ny, edge, group,
    loads_ref, flex_hbm, schur_hbm, couple_ref, perm_ref, cinv_ref,
    mult_ref, resid_ref,
    flex_v, flex_hi, flex_lo, schur_v, cpad, ck_hi, ck_lo, solve_hi, solve_lo,
    pick, cpl_hi, cpl_lo, cown, cnear, bt,
    recv, send, own_a, own_b, first, own_c, second,
    u_ref, u_hi, u_lo, r_ref, s_ref, p_ref,
    flex_sem, schur_sem, cs_sem, cr_sem, ex_send, ex_recv, f_send, f_recv, g_send, g_recv,
):
    i = lax.axis_index("sx")
    j = lax.axis_index("sy")
    exists = (i > 0, i < nx - 1, j > 0, j < ny - 1)
    near = tuple((i + di, j + dj) for di, dj in NEAR)
    kdim = ny * group

    def rows(e):
        return pl.ds(e * edge, edge)

    def flex_copy(e):
        return pltpu.make_async_copy(flex_hbm.at[rows(e)], flex_v.at[rows(e)], flex_sem.at[e])

    for e in range(4):
        flex_copy(e).start()
    schur_copy = pltpu.make_async_copy(schur_hbm, schur_v, schur_sem)
    schur_copy.start()

    barrier = pltpu.get_barrier_semaphore()

    @pl.loop(1, nx)
    def _(d):
        pl.semaphore_signal(barrier, inc=1, device_id=(lax.rem(i + d, nx), j), device_id_type=MESH)

    @pl.when(j < ny - 1)
    def _():
        @pl.loop(0, nx)
        def _(d):
            pl.semaphore_signal(barrier, inc=1, device_id=(d, j + 1), device_id_type=MESH)

    @pl.loop(0, ny)
    def _(d):
        @pl.when((d != j) & (d != j + 1))
        def _():
            pl.semaphore_signal(barrier, inc=1, device_id=(i, d), device_id_type=MESH)

    nc = cinv_ref.shape[0]
    cpad[...] = jnp.zeros_like(cpad)
    cpad[0:nc, 0:nc] = cinv_ref[...]
    order = jnp.where(iota((cpad.shape[0], kdim), 0) == perm_ref[...], 1.0, 0.0).astype(BF16)
    m_rows = solve_hi.shape[0]
    m_id = iota((m_rows, kdim), 0)
    col = iota((m_rows, kdim), 1)
    corner_p = i - 1 + (m_id >> 2)
    corner_q = j - 1 + (m_id & 3)
    inside = (m_id < 16) & (corner_p >= 1) & (corner_p <= nx - 1) & (corner_q >= 1) & (corner_q <= ny - 1)
    wanted = group * (corner_q - 1) + corner_p - 1
    select = jnp.where(inside & (col == wanted), 1.0, 0.0).astype(BF16)
    col_in = col - group * ((col * (65536 // group + 1)) >> 16)
    totals = jnp.where((m_id >= 16) & (col_in == m_id - 16 + group - 8), 1.0, 0.0)
    c_high, c_low = halves(cpad[...])
    contract0 = (((0,), (0,)), ((), ()))
    for part, out, solve in ((c_high, ck_hi, solve_hi), (c_low, ck_lo, solve_lo)):
        right = dot(part, order).astype(BF16)
        out[...] = lax.dot_general(order, right, contract0, preferred_element_type=F32).astype(BF16)
        solve[...] = (dot(select, out[...]) + (totals if out is ck_hi else 0.0)).astype(BF16)

    pm = iota(pick.shape, 0)
    pn = iota(pick.shape, 1)
    slot = pn >> 3
    row = pn & 7
    source = slot - jnp.where(slot >= nx, nx, 0)
    corner_row = (pm < nx - 1) & (row < 2) & (source + row == pm + 1)
    scalar_row = (pm >= group - 8) & (slot < nx) & (row >= 2) & (row - 2 == pm - (group - 8))
    pick[...] = jnp.where(corner_row | scalar_row, 1.0, 0.0).astype(BF16)

    couple_all = couple_ref[...]
    zero6 = jnp.zeros((6, couple_all.shape[1]), F32)
    stacked = jnp.concatenate(
        [couple_all[1:2], couple_all[3:4], zero6, couple_all[0:1], couple_all[2:3], zero6], 0
    )
    cpl_hi[...], cpl_lo[...] = halves(stacked)
    for e in range(4):
        cown[e] = jnp.concatenate(
            [couple_all[:, e * edge : (e + 1) * edge], jnp.zeros((4, edge), F32)], 0
        )
    s_ref[...] = jnp.zeros_like(s_ref)
    p_ref[...] = jnp.zeros_like(p_ref)
    mult_ref[...] = jnp.zeros_like(mult_ref)

    @pl.when(j == ny - 1)
    def _():
        first[:, nx:, :, :] = jnp.zeros((ITERS + 1, nx, 8, first.shape[-1]), F32)

    sends_to = (nx - 1) + (ny - 1)

    @pl.when(j > 0)
    def _():
        pl.semaphore_wait(barrier, sends_to + nx - 1)

    @pl.when(j == 0)
    def _():
        pl.semaphore_wait(barrier, sends_to)

    def couple_copy(e):
        return pltpu.make_async_remote_copy(
            src_ref=cown.at[e], dst_ref=cnear.at[OPPOSITE[e]],
            send_sem=cs_sem.at[e], recv_sem=cr_sem.at[OPPOSITE[e]],
            device_id=near[e], device_id_type=MESH,
        )

    def couple_arrival(e):
        return pltpu.make_async_remote_copy(
            src_ref=cown.at[e], dst_ref=cnear.at[e],
            send_sem=cs_sem.at[e], recv_sem=cr_sem.at[e],
            device_id=near[e], device_id_type=MESH,
        )

    for e in range(4):
        pl.when(exists[e])(lambda e=e: couple_copy(e).start())

    def edge_copy(t, e):
        return pltpu.make_async_remote_copy(
            src_ref=send.at[t, e], dst_ref=recv.at[t, OPPOSITE[e]],
            send_sem=ex_send.at[t, e], recv_sem=ex_recv.at[t, OPPOSITE[e]],
            device_id=near[e], device_id_type=MESH,
        )

    def edge_arrival(t, e):
        return pltpu.make_async_remote_copy(
            src_ref=send.at[t, e], dst_ref=recv.at[t, e],
            send_sem=ex_send.at[t, e], recv_sem=ex_recv.at[t, e],
            device_id=near[e], device_id_type=MESH,
        )

    def corner_partials(with_low):
        if with_low:
            return dot3(cpl_hi[...], cpl_lo[...], u_hi[...], u_lo[...])
        return dot(cpl_hi[...], u_hi[...]) + dot(cpl_lo[...], u_hi[...])

    def first_stage(k, partial, scalars):
        row_id = iota((8, partial.shape[1]), 0)
        message = partial[0:8]
        for n, value in enumerate(scalars):
            message = jnp.where(row_id == n + 2, value, message)
        own_a[k] = message
        own_b[k] = partial[8:16]
        first[k, i] = message

        @pl.loop(1, nx)
        def _(d):
            pltpu.make_async_remote_copy(
                src_ref=own_a.at[k], dst_ref=first.at[k, i],
                send_sem=f_send.at[k], recv_sem=f_recv.at[k],
                device_id=(lax.rem(i + d, nx), j), device_id_type=MESH,
            ).start()

        @pl.when(j > 0)
        def _():
            @pl.loop(0, nx)
            def _(d):
                pltpu.make_async_remote_copy(
                    src_ref=own_b.at[k], dst_ref=first.at[k, nx + i],
                    send_sem=f_send.at[k], recv_sem=f_recv.at[k],
                    device_id=(lax.rem(i + d, nx), j - 1), device_id_type=MESH,
                ).start()

    def bytes_of(ref, sem):
        return pltpu.make_async_copy(ref, ref, sem)

    def second_stage(k):
        @pl.when(j < ny - 1)
        def _():
            bytes_of(first.at[k, pl.ds(0, 2 * nx - 1)], f_recv.at[k]).wait()

        @pl.when(j == ny - 1)
        def _():
            bytes_of(first.at[k, pl.ds(0, nx - 1)], f_recv.at[k]).wait()

        got_high, got_low = halves(first[k].reshape(2 * nx * 8, first.shape[-1]))
        summed = dot(pick[...], got_high) + dot(pick[...], got_low)
        own_c[k] = summed
        second[k, j] = summed

        @pl.loop(1, ny)
        def _(d):
            pltpu.make_async_remote_copy(
                src_ref=own_c.at[k], dst_ref=second.at[k, j],
                send_sem=g_send.at[k], recv_sem=g_recv.at[k],
                device_id=(i, lax.rem(j + d, ny)), device_id_type=MESH,
            ).start()

    def coarse_solve(k, with_energy):
        bytes_of(second.at[k, pl.ds(0, ny - 1)], g_recv.at[k]).wait()
        gathered = second[k].reshape(kdim, second.shape[-1])
        g_high, g_low = halves(gathered)
        local = dot3(solve_hi[...], solve_lo[...], g_high, g_low)
        z_high, z_low = halves(local[0:16])
        z_stack = jnp.concatenate([z_high, z_low, z_high], 0)
        energy = None
        if with_energy:
            energy = colsum(gathered * dot3(ck_hi[...], ck_lo[...], g_high, g_low))
        return z_stack, local[16:24], energy

    def flex_products(k, e_list, last):
        energy = 0.0
        for e in e_list:
            product = dot(flex_hi[rows(e)], u_hi[...]) + dot(flex_lo[rows(e)], u_hi[...])
            send[k, e] = product
            if e in (0, 2):
                pl.when(exists[e])(lambda e=e: edge_copy(k, e).start())
            else:
                pl.when(exists[e] & jnp.logical_not(last))(lambda e=e: edge_copy(k, e).start())
            energy = energy + colsum(u_ref[e] * product)
        return energy

    loads = loads_ref[...]
    u_hi[...] = loads
    for e in range(4):
        u_ref[e] = loads[e * edge : (e + 1) * edge].astype(F32)
    zero_row = jnp.zeros((1, loads.shape[1]), F32)
    first_stage(0, corner_partials(False), (zero_row, zero_row, zero_row))
    for e in range(4):
        flex_copy(e).wait()
        flex_hi[rows(e)], flex_lo[rows(e)] = halves(flex_v[rows(e)])
        flex_products(0, (e,), False)
    schur_copy.wait()
    second_stage(0)

    for e in range(4):
        bt[rows(e)] = jnp.zeros((edge, 48), BF16)

        def build(e=e):
            couple_arrival(e).wait_recv()
            kk = iota((8, 48), 0)
            corner = iota((8, 48), 1) & 15

            def placed(dp, dq):
                at = 4 * (dp + (kk >> 1)) + dq + (kk & 1)
                return jnp.where((corner == at) & (kk < 4), 1.0, 0.0)

            di, dj = NEAR[e]
            highest = lax.Precision.HIGHEST
            mixed = jnp.dot(cown[e].T, placed(1, 1), precision=highest) - jnp.dot(
                cnear[e].T, placed(1 + di, 1 + dj), precision=highest
            )
            high, low = halves(mixed)
            bt[rows(e)] = jnp.where(
                iota(mixed.shape, 1) < 32, high.astype(F32), low.astype(F32)
            ).astype(BF16)

        pl.when(exists[e])(build)

    z_stack, _, _ = coarse_solve(0, False)
    for e in range(4):
        r_ref[e] = jnp.zeros(r_ref.shape[1:], F32)

        def arrived(e=e):
            edge_arrival(0, e).wait_recv()
            r_ref[e] = send[0, e] - recv[0, e] + dot(bt[rows(e)], z_stack)

        pl.when(exists[e])(arrived)

    def iteration(k, carry):
        rz_old, energy_old = carry
        last = k == ITERS
        t = ITERS + k
        for e in range(4):
            u_hi[rows(e)] = (0.5 * r_ref[e]).astype(BF16)
        for e in range(4):
            send[t, e] = 0.5 * dot(schur_v[rows(e)], u_hi[...])
            pl.when(exists[e])(lambda e=e: edge_copy(t, e).start())
        for e in range(4):
            u_ref[e] = jnp.zeros(u_ref.shape[1:], F32)

            def arrived(e=e):
                edge_arrival(t, e).wait_recv()
                u_ref[e] = send[t, e] - recv[t, e]

            pl.when(exists[e])(arrived)
            u_hi[rows(e)], u_lo[rows(e)] = halves(u_ref[e])
        rz_part = 0.5 * sum(colsum(r_ref[e] * u_ref[e]) for e in range(4))
        cross_part = 0.5 * sum(colsum(s_ref[e] * u_ref[e]) for e in range(4))
        partial = corner_partials(True)
        flex_part = flex_products(k, range(4), last)
        first_stage(k, partial, (rz_part, cross_part, flex_part))
        second_stage(k)
        z_stack, totals, coarse_part = coarse_solve(k, True)
        rz = totals[0:1]
        cross = totals[1:2]
        beta = jnp.where(k == 1, 0.0, rz / rz_old)
        energy = totals[2:3] + coarse_part + beta * (2.0 * cross + beta * energy_old)
        step = rz / energy
        for n, e in enumerate((1, 3)):
            direction = u_ref[e] + beta * p_ref[n]
            p_ref[n] = direction
            mult_ref[n] = mult_ref[n] + step * direction
        for e in range(4):

            def arrived(e=e):
                edge_arrival(k, e).wait_recv()
                image = send[k, e] - recv[k, e] + dot(bt[rows(e)], z_stack)
                image = image + beta * s_ref[e]
                s_ref[e] = image
                r_ref[e] = r_ref[e] - step * image

            if e in (1, 3):
                pl.when(exists[e])(arrived)
            else:
                pl.when(exists[e] & jnp.logical_not(last))(arrived)
        return rz, energy

    lax.fori_loop(1, ITERS + 1, iteration, (zero_row + 1.0, zero_row))
    resid_ref[0] = r_ref[1]
    resid_ref[1] = r_ref[3]

    for e in range(4):
        pl.when(exists[e])(lambda e=e: couple_copy(e).wait_send())

    @pl.loop(0, 2 * ITERS + 1)
    def _(t):
        for e in range(4):
            if e in (0, 2):
                pl.when(exists[e])(lambda e=e: edge_copy(t, e).wait_send())
            else:
                pl.when(exists[e] & (t != ITERS))(lambda e=e: edge_copy(t, e).wait_send())

    @pl.loop(0, ITERS + 1)
    def _(k):
        @pl.when(j > 0)
        def _():
            bytes_of(first.at[k, pl.ds(0, 2 * nx - 1)], f_send.at[k]).wait()

        @pl.when(j == 0)
        def _():
            bytes_of(first.at[k, pl.ds(0, nx - 1)], f_send.at[k]).wait()

        bytes_of(second.at[k, pl.ds(0, ny - 1)], g_send.at[k]).wait()


def per_device(loads, flex, schur, couple, corner_perm, coarse_inverse):
    nx = lax.axis_size("sx")
    ny = lax.axis_size("sy")
    iface, cols = loads.shape[2:]
    edge = iface // 4
    nc = coarse_inverse.shape[0]
    ncp = -(-nc // 128) * 128
    group = -(-(nx - 1) // 8) * 8 + 8
    kdim = ny * group
    perm = corner_perm.reshape(nx - 1, ny - 1).T
    perm = jnp.pad(perm, ((0, 1), (0, group - (nx - 1))), constant_values=-1).reshape(1, kdim)
    steps = 2 * ITERS + 1
    rounds = ITERS + 1
    vmem = pl.BlockSpec(memory_space=pltpu.VMEM)
    hbm = pl.BlockSpec(memory_space=pl.ANY)
    dma = pltpu.SemaphoreType.DMA
    out = jax.ShapeDtypeStruct((2, edge, cols), F32)
    mult, resid = pl.pallas_call(
        functools.partial(kernel, nx, ny, edge, group),
        out_shape=(out, out),
        in_specs=[vmem, hbm, hbm, vmem, vmem, vmem],
        out_specs=(vmem, vmem),
        scratch_shapes=[
            pltpu.VMEM((iface, iface), F32),
            pltpu.VMEM((iface, iface), BF16),
            pltpu.VMEM((iface, iface), BF16),
            pltpu.VMEM((iface, iface), BF16),
            pltpu.VMEM((ncp, ncp), F32),
            pltpu.VMEM((kdim, kdim), BF16),
            pltpu.VMEM((kdim, kdim), BF16),
            pltpu.VMEM((24, kdim), BF16),
            pltpu.VMEM((24, kdim), BF16),
            pltpu.VMEM((group, 2 * nx * 8), BF16),
            pltpu.VMEM((16, iface), BF16),
            pltpu.VMEM((16, iface), BF16),
            pltpu.VMEM((4, 8, edge), F32),
            pltpu.VMEM((4, 8, edge), F32),
            pltpu.VMEM((iface, 48), BF16),
            pltpu.VMEM((steps, 4, edge, cols), F32),
            pltpu.VMEM((steps, 4, edge, cols), F32),
            pltpu.VMEM((rounds, 8, cols), F32),
            pltpu.VMEM((rounds, 8, cols), F32),
            pltpu.VMEM((rounds, 2 * nx, 8, cols), F32),
            pltpu.VMEM((rounds, group, cols), F32),
            pltpu.VMEM((rounds, ny, group, cols), F32),
            pltpu.VMEM((4, edge, cols), F32),
            pltpu.VMEM((iface, cols), BF16),
            pltpu.VMEM((iface, cols), BF16),
            pltpu.VMEM((4, edge, cols), F32),
            pltpu.VMEM((4, edge, cols), F32),
            pltpu.VMEM((2, edge, cols), F32),
            dma((4,)),
            dma,
            dma((4,)),
            dma((4,)),
            dma((steps, 4)),
            dma((steps, 4)),
            dma((rounds,)),
            dma((rounds,)),
            dma((rounds,)),
            dma((rounds,)),
        ],
        compiler_params=pltpu.CompilerParams(
            collective_id=0, has_side_effects=True, vmem_limit_bytes=48 * 1024 * 1024
        ),
    )(loads[0, 0], flex[0, 0], schur[0, 0], couple[0, 0], perm, coarse_inverse)
    return mult[None, None], resid[None, None]


def solution(mesh):
    placed = (
        P("sx", "sy", None, None),
        P("sx", "sy", None, None),
        P("sx", "sy", None, None),
        P("sx", "sy", None, None),
        P(),
        P(),
    )
    return jax.shard_map(
        per_device,
        mesh=mesh,
        in_specs=placed,
        out_specs=(P("sx", "sy", None, None, None), P("sx", "sy", None, None, None)),
        check_vma=False,
    )
```

time: 2030 us -> 138 us (0.07)
  waiting for transfers between devices: 1290 us -> 0 us
  blocking collectives: 563 us -> 0 us
  Pallas kernels: 0 us -> 130 us
  starting transfers between devices: 80.4 us -> 0 us
  matrix products: 52.4 us -> 0 us
  other arithmetic: 23.9 us -> 0 us
    psum x5 -> x0, waiting for transfers between devices: 1230 us -> none  [correction(): lax.psum(jnp.dot(own_table, partial_value, precision=highest), ('sx', 'sy'))]
    psum x7 -> x0, blocking collectives: 563 us -> none  [the longest x4 328 us: residual_product(): return lax.psum(local_inner(resid, pre_vec), ('sx', 'sy'))]
    pallas_call x0 -> x1, Pallas kernels: none -> 130 us  [per_device(): pl.pallas_call(functools.partial(kernel, nx, ny, edge, group), out_shape=...]
    ppermute x34 -> x0, starting transfers between devices: 80 us -> none  [passed_along(): return lax.ppermute(x, axis, pairs)]
    ppermute x34 -> x0, waiting for transfers between devices: 66.9 us -> none  [passed_along(): return lax.ppermute(x, axis, pairs)]
    dot_general x30 -> x0, matrix products: 52.4 us -> none  [the longest x5 25.5 us: operator_local(): local_part = jnp.dot(flex_local, vec_f32, precision=highest)]
  transfers between devices with their start and end apart: 39 -> 0, of which waited for: 36 -> 0; matrix products, arithmetic and copies ran while one was open for 0% -> 0% of each run, Pallas kernels for 0% -> 0%
where the time goes in v1:
time: 138 us
  Pallas kernels  130 us (94%)
  local copies, waits for them, and re-layouts  6.56 us (5%)
    pallas_call x1, Pallas kernels, per_device(): pl.pallas_call(functools.partial(kernel, nx, ny, edge, group), out_shape=...  130 us
    unnamed x11, local copies, waits for them, and re-layouts  5.7 us

profile of v1, /device:TPU:1, one launch (start us, length us, event | category | flops | bytes accessed | tf_op | source)
XLA Modules:
  0.0 137.6 jit_solution(10868083279109413400)
XLA Ops:
  0.6 0.8 reshape.10
  1.4 0.1 copy.9
  1.5 0.1 reshape.11.perm_ref
  1.6 0.0 copy-start
  1.6 1.6 %copy-done = bf16[1,1,1024,1024]{3,2,1,0:T(8,128)(2,1)S(1)} copy-done((bf16[1,1,1024,1024]{3,2,1,0:T(8,128)(2,1)S(1)}, bf16[1,1,1024,1024]{3,2,1,0:T(8,128)(2,1)}, u32[]{:S(2)}) %copy-start) | copy-done | bytes 2097176
  3.2 0.0 copy-start.1
  3.2 0.9 copy-done.1
  4.1 0.0 copy-start.2
  4.1 0.9 copy-done.2
  5.1 0.0 copy-start.3
  5.1 0.7 copy-done.3
  5.8 130.4 %shard_map.77 = (f32[2,256,128]{2,1,0:T(8,128)S(1)}, f32[2,256,128]{2,1,0:T(8,128)S(1)}) custom-call(bf16[1024,128]{1,0:T(8,128)(2,1)S(1)} %bitcast.8, f32[1024,1024]{1,0:T(8,128)} %bitcast.12, bf16[1024,1024]{1,0:T(8,128)(2,1)S(1)} %bitcast.7, f32[4,1024]{1,0:T(4,128)S(1)} %bitcast.11, s32[1,384]{1,0:T(1,128)S(1)} %reshape.11.perm_ref, f32[225,225]{1,0:T(8,128)S(1)} %copy-done.2), custom_call_target="tpu_custom_call" | custom-call | tf_op jit(solution)/shard_map/pallas_call | solution.py:395
  136.2 0.7 copy.12
  136.9 0.7 copy.13
  (1 shorter events, 0.0 us)
Async XLA Ops:
  1.6 1.6 %copy-start = (bf16[1,1,1024,1024]{3,2,1,0:T(8,128)(2,1)S(1)}, bf16[1,1,1024,1024]{3,2,1,0:T(8,128)(2,1)}, u32[]{:S(2)}) copy-start(bf16[1,1,1024,1024]{3,2,1,0:T(8,128)(2,1)} %param.8) | copy-start | bytes 6291460
  3.2 0.9 copy-start.1
  4.1 0.9 copy-start.2
  5.1 0.7 copy-start.3

commit v2 on v1

v2 whole, which is shorter than its diff:
```python
import functools

import jax
import jax.numpy as jnp
from jax import lax
from jax.experimental import pallas as pl
from jax.experimental.pallas import tpu as pltpu
from jax.sharding import PartitionSpec as P

ITERS = 4
ZROWS = 48
MESH = pl.DeviceIdType.MESH
F32 = jnp.float32
BF16 = jnp.bfloat16
OPPOSITE = (1, 0, 3, 2)
NEAR = ((-1, 0), (1, 0), (0, -1), (0, 1))


def dot(a, b):
    return jnp.dot(a, b, preferred_element_type=F32)


def halves(x):
    high = x.astype(BF16)
    return high, (x - high.astype(F32)).astype(BF16)


def dot3(a_high, a_low, b_high, b_low):
    return dot(a_high, b_high) + (dot(a_high, b_low) + dot(a_low, b_high))


def colsum(x):
    return jnp.sum(x, axis=0, keepdims=True)


def iota(shape, dim):
    return lax.broadcasted_iota(jnp.int32, shape, dim)


def kernel(
    nx, ny, edge, group,
    loads_ref, flex_hbm, schur_hbm, couple_ref, perm_ref, cinv_ref,
    mult_ref, resid_ref,
    flex_v, flex_2, schur_v, cpad, ck_2, solve_2,
    pick, cpl_2, cown, cnear, b_rows, bt, g_rows, g_near, mbt,
    recv, send, own_a, own_b, first, own_c, second,
    u_ref, weights, z_ref, r_ref, s_ref, q_ref, p_ref,
    flex_sem, schur_sem, cs_sem, cr_sem, gs_sem, gr_sem,
    ex_send, ex_recv, f_send, f_recv, g_send, g_recv,
):
    i = lax.axis_index("sx")
    j = lax.axis_index("sy")
    exists = (i > 0, i < nx - 1, j > 0, j < ny - 1)
    near = tuple((i + di, j + dj) for di, dj in NEAR)
    kdim = ny * group
    cols = loads_ref.shape[1]
    highest = lax.Precision.HIGHEST

    def rows(e):
        return pl.ds(e * edge, edge)

    def flex_copy(e):
        return pltpu.make_async_copy(flex_hbm.at[rows(e)], flex_v.at[rows(e)], flex_sem.at[e])

    for e in range(4):
        flex_copy(e).start()
    schur_copy = pltpu.make_async_copy(schur_hbm, schur_v, schur_sem)
    schur_copy.start()

    barrier = pltpu.get_barrier_semaphore()

    @pl.loop(1, nx)
    def _(d):
        pl.semaphore_signal(barrier, inc=1, device_id=(lax.rem(i + d, nx), j), device_id_type=MESH)

    @pl.when(j < ny - 1)
    def _():
        @pl.loop(0, nx)
        def _(d):
            pl.semaphore_signal(barrier, inc=1, device_id=(d, j + 1), device_id_type=MESH)

    @pl.loop(0, ny)
    def _(d):
        @pl.when((d != j) & (d != j + 1))
        def _():
            pl.semaphore_signal(barrier, inc=1, device_id=(i, d), device_id_type=MESH)

    couple_all = couple_ref[...]
    zero6 = jnp.zeros((6, couple_all.shape[1]), F32)
    stacked = jnp.concatenate(
        [couple_all[1:2], couple_all[3:4], zero6, couple_all[0:1], couple_all[2:3], zero6], 0
    )
    cpl_2[0:16], cpl_2[16:32] = halves(stacked)
    for e in range(4):
        cown[e] = jnp.concatenate(
            [couple_all[:, e * edge : (e + 1) * edge], jnp.zeros((4, edge), F32)], 0
        )

    pm = iota(pick.shape, 0)
    pn = iota(pick.shape, 1)
    slot = pn >> 3
    row = pn & 7
    source = slot - jnp.where(slot >= nx, nx, 0)
    corner_row = (pm < nx - 1) & (row < 2) & (source + row == pm + 1)
    scalar_row = (pm >= group - 8) & (slot < nx) & (row >= 2) & (row - 2 == pm - (group - 8))
    pick[...] = jnp.where(corner_row | scalar_row, 1.0, 0.0).astype(BF16)

    for ref in (r_ref, s_ref, q_ref, p_ref, mult_ref, u_ref):
        ref[...] = jnp.zeros_like(ref)

    @pl.when(j == ny - 1)
    def _():
        first[:, nx:, :, :] = jnp.zeros((ITERS + 1, nx, 8, cols), F32)

    def coarse_operator():
        nc = cinv_ref.shape[0]
        cpad[...] = jnp.zeros_like(cpad)
        cpad[0:nc, 0:nc] = cinv_ref[...]
        order = jnp.where(iota((cpad.shape[0], kdim), 0) == perm_ref[...], 1.0, 0.0).astype(BF16)
        m_id = iota((ZROWS + 8, kdim), 0)
        col = iota((ZROWS + 8, kdim), 1)
        block_row = (m_id * 43) >> 8
        corner_p = i - 2 + block_row
        corner_q = j - 2 + m_id - 6 * block_row
        inside = (m_id < 36) & (corner_p >= 1) & (corner_p <= nx - 1)
        inside = inside & (corner_q >= 1) & (corner_q <= ny - 1)
        wanted = group * (corner_q - 1) + corner_p - 1
        select = jnp.where(inside & (col == wanted), 1.0, 0.0).astype(BF16)
        col_in = col - group * ((col * (65536 // group + 1)) >> 16)
        totals = jnp.where((m_id >= ZROWS) & (col_in == m_id - ZROWS + group - 8), 1.0, 0.0)
        contract0 = (((0,), (0,)), ((), ()))
        for n, part in enumerate(halves(cpad[...])):
            right = dot(part, order).astype(BF16)
            full = lax.dot_general(order, right, contract0, preferred_element_type=F32).astype(BF16)
            ck_2[n] = full
            solve_2[n] = (dot(select, full) + (totals if n == 0 else 0.0)).astype(BF16)

    def couple_copy(e):
        return pltpu.make_async_remote_copy(
            src_ref=cown.at[e], dst_ref=cnear.at[OPPOSITE[e]],
            send_sem=cs_sem.at[e], recv_sem=cr_sem.at[OPPOSITE[e]],
            device_id=near[e], device_id_type=MESH,
        )

    def couple_arrival(e):
        return pltpu.make_async_remote_copy(
            src_ref=cown.at[e], dst_ref=cnear.at[e],
            send_sem=cs_sem.at[e], recv_sem=cr_sem.at[e],
            device_id=near[e], device_id_type=MESH,
        )

    def image_copy(e):
        return pltpu.make_async_remote_copy(
            src_ref=g_rows.at[e, pl.ds(0, 32)], dst_ref=g_near.at[OPPOSITE[e], pl.ds(0, 32)],
            send_sem=gs_sem.at[e], recv_sem=gr_sem.at[OPPOSITE[e]],
            device_id=near[e], device_id_type=MESH,
        )

    def image_arrival(e):
        return pltpu.make_async_remote_copy(
            src_ref=g_rows.at[e, pl.ds(0, 32)], dst_ref=g_near.at[e, pl.ds(0, 32)],
            send_sem=gs_sem.at[e], recv_sem=gr_sem.at[e],
            device_id=near[e], device_id_type=MESH,
        )

    def edge_copy(t, e):
        return pltpu.make_async_remote_copy(
            src_ref=send.at[t, e], dst_ref=recv.at[t, OPPOSITE[e]],
            send_sem=ex_send.at[t, e], recv_sem=ex_recv.at[t, OPPOSITE[e]],
            device_id=near[e], device_id_type=MESH,
        )

    def edge_arrival(t, e):
        return pltpu.make_async_remote_copy(
            src_ref=send.at[t, e], dst_ref=recv.at[t, e],
            send_sem=ex_send.at[t, e], recv_sem=ex_recv.at[t, e],
            device_id=near[e], device_id_type=MESH,
        )

    def bytes_of(ref, sem):
        return pltpu.make_async_copy(ref, ref, sem)

    def set_weights(e, value):
        weights[rows(e), 0:cols], weights[rows(e), cols:] = halves(value)

    def corner_partials():
        product = dot(cpl_2[...], weights[...])
        product = product[0:16] + product[16:32]
        return product[:, :cols] + product[:, cols:]

    def flex_products(k, e, last=False):
        product = dot(flex_2[e], weights[...])
        product = product[:edge] + product[edge:]
        product = product[:, :cols] + product[:, cols:]
        send[k, e] = product
        if e in (0, 2) or not last:
            pl.when(exists[e])(lambda: edge_copy(k, e).start())
        return colsum(u_ref[e] * product)

    def schur_products(t):
        for e in range(4):
            product = dot(schur_v[rows(e)], weights[...])
            send[t, e] = 0.5 * (product[:, :cols] + product[:, cols:])
            pl.when(exists[e])(lambda e=e: edge_copy(t, e).start())

    def first_stage(k, partial, scalars):
        row_id = iota((8, cols), 0)
        message = partial[0:8]
        for n, value in enumerate(scalars):
            message = jnp.where(row_id == n + 2, value, message)
        own_a[k] = message
        own_b[k] = partial[8:16]
        first[k, i] = message

        @pl.loop(1, nx)
        def _(d):
            pltpu.make_async_remote_copy(
                src_ref=own_a.at[k], dst_ref=first.at[k, i],
                send_sem=f_send.at[k], recv_sem=f_recv.at[k],
                device_id=(lax.rem(i + d, nx), j), device_id_type=MESH,
            ).start()

        @pl.when(j > 0)
        def _():
            @pl.loop(0, nx)
            def _(d):
                pltpu.make_async_remote_copy(
                    src_ref=own_b.at[k], dst_ref=first.at[k, nx + i],
                    send_sem=f_send.at[k], recv_sem=f_recv.at[k],
                    device_id=(lax.rem(i + d, nx), j - 1), device_id_type=MESH,
                ).start()

    def second_stage(k):
        @pl.when(j < ny - 1)
        def _():
            bytes_of(first.at[k, pl.ds(0, 2 * nx - 1)], f_recv.at[k]).wait()

        @pl.when(j == ny - 1)
        def _():
            bytes_of(first.at[k, pl.ds(0, nx - 1)], f_recv.at[k]).wait()

        got_high, got_low = halves(first[k].reshape(2 * nx * 8, cols))
        summed = dot(pick[...], got_high) + dot(pick[...], got_low)
        own_c[k] = summed
        second[k, j] = summed

        @pl.loop(1, ny)
        def _(d):
            pltpu.make_async_remote_copy(
                src_ref=own_c.at[k], dst_ref=second.at[k, j],
                send_sem=g_send.at[k], recv_sem=g_recv.at[k],
                device_id=(i, lax.rem(j + d, ny)), device_id_type=MESH,
            ).start()

    def coarse_solve(k, with_energy):
        bytes_of(second.at[k, pl.ds(0, ny - 1)], g_recv.at[k]).wait()
        gathered = second[k].reshape(kdim, cols)
        g_high, g_low = halves(gathered)
        local = dot3(solve_2[0], solve_2[1], g_high, g_low)
        z_high, z_low = halves(local[0:ZROWS])
        z_ref[0:ZROWS] = z_high
        z_ref[ZROWS : 2 * ZROWS] = z_low
        z_ref[2 * ZROWS :] = z_high
        energy = None
        if with_energy:
            energy = colsum(gathered * dot3(ck_2[0], ck_2[1], g_high, g_low))
        return local[ZROWS : ZROWS + 8], energy

    def scalars_of(k, rz_old, energy_old):
        totals, coarse_part = coarse_solve(k, True)
        rz = totals[0:1]
        beta = jnp.where(k == 1, 0.0, rz / rz_old)
        energy = totals[2:3] + coarse_part + beta * (2.0 * totals[1:2] + beta * energy_old)
        return rz, energy, beta, rz / energy

    def triple(x):
        high, low = halves(x)
        high = high.astype(F32)
        return jnp.concatenate([high, high, low.astype(F32)], 0).T.astype(BF16)

    def precondition_edges(k, t):
        for e in range(4):
            weights[rows(e)] = jnp.zeros((edge, 2 * cols), BF16)

            def arrived(e=e):
                edge_arrival(k, e).wait_recv()
                set_weights(e, 0.5 * (send[k, e] - recv[k, e]))

            pl.when(exists[e])(arrived)
        schur_products(t)

    loads = loads_ref[...]
    weights[:, 0:cols] = loads
    weights[:, cols:] = jnp.zeros_like(loads)
    zero_row = jnp.zeros((1, cols), F32)

    sends_to = (nx - 1) + (ny - 1)

    @pl.when(j > 0)
    def _():
        pl.semaphore_wait(barrier, sends_to + nx - 1)

    @pl.when(j == 0)
    def _():
        pl.semaphore_wait(barrier, sends_to)

    for e in range(4):
        pl.when(exists[e])(lambda e=e: couple_copy(e).start())
    for e in range(4):
        flex_copy(e).wait()
        flex_2[e, 0:edge], flex_2[e, edge:] = halves(flex_v[rows(e)])
        flex_products(0, e)
    first_stage(0, corner_partials(), ())

    coarse_operator()
    for e in range(4):
        b_rows[:, rows(e)] = jnp.zeros((ZROWS, edge), F32)

        def build(e=e):
            couple_arrival(e).wait_recv()
            corner = iota((ZROWS, 8), 0)
            kk = iota((ZROWS, 8), 1)

            def placed(dp, dq):
                at = 6 * (dp + (kk >> 1)) + dq + (kk & 1)
                return jnp.where((corner == at) & (kk < 4), 1.0, 0.0)

            di, dj = NEAR[e]
            b_rows[:, rows(e)] = jnp.dot(placed(2, 2), cown[e], precision=highest) - jnp.dot(
                placed(2 + di, 2 + dj), cnear[e], precision=highest
            )

        pl.when(exists[e])(build)
        bt[rows(e)] = triple(b_rows[:, rows(e)])

    schur_copy.wait()
    precondition_edges(0, ITERS + 1)
    b_high, b_low = halves(b_rows[...])
    contract1 = (((1,), (1,)), ((), ()))
    for e in range(4):
        g_rows[e] = 0.25 * (
            lax.dot_general(b_high, schur_v[rows(e)], contract1, preferred_element_type=F32)
            + lax.dot_general(b_low, schur_v[rows(e)], contract1, preferred_element_type=F32)
        )
        pl.when(exists[e])(lambda e=e: image_copy(e).start())
    second_stage(0)
    for e in range(4):

        def build(e=e):
            image_arrival(e).wait_recv()
            shift = 6 * NEAR[e][0] + NEAR[e][1]
            other = jnp.concatenate([g_near[e, 0:32], jnp.zeros((ZROWS - 32, edge), F32)], 0)
            other = pltpu.roll(other, shift % ZROWS, 0)
            mbt[rows(e)] = triple(g_rows[e] - other)

        pl.when(exists[e])(build)
    coarse_solve(0, False)
    for e in range(4):
        weights[rows(e)] = jnp.zeros((edge, 2 * cols), BF16)

        def arrived(e=e):
            edge_arrival(ITERS + 1, e).wait_recv()
            value = send[ITERS + 1, e] - recv[ITERS + 1, e] + dot(mbt[rows(e)], z_ref[...])
            u_ref[e] = value
            set_weights(e, value)

        pl.when(exists[e])(arrived)

    def open_iteration(k, beta, step, last):
        flex_part = sum(flex_products(k, e, last) for e in range(4))
        for e in range(4):

            def update(e=e):
                image = send[k - 1, e] - recv[k - 1, e] + dot(bt[rows(e)], z_ref[...])
                image = image + beta * s_ref[e]
                s_ref[e] = image
                r_ref[e] = r_ref[e] - step * image

            pl.when(exists[e])(update)
        rz_part = 0.5 * sum(colsum(r_ref[e] * u_ref[e]) for e in range(4))
        cross_part = 0.5 * sum(colsum(s_ref[e] * u_ref[e]) for e in range(4))
        first_stage(k, corner_partials(), (rz_part, cross_part, flex_part))

    def step_along(beta, step):
        for n, e in enumerate((1, 3)):
            direction = u_ref[e] + beta * p_ref[n]
            p_ref[n] = direction
            mult_ref[n] = mult_ref[n] + step * direction

    def iteration(k, carry):
        rz, energy, beta, step = carry
        t = ITERS + 1 + k
        open_iteration(k, beta, step, False)
        precondition_edges(k, t)
        second_stage(k)
        rz, energy, beta, step = scalars_of(k, rz, energy)
        step_along(beta, step)
        for e in range(4):
            weights[rows(e)] = jnp.zeros((edge, 2 * cols), BF16)

            def arrived(e=e):
                edge_arrival(t, e).wait_recv()
                image = send[t, e] - recv[t, e] + dot(mbt[rows(e)], z_ref[...])
                image = image + beta * q_ref[e]
                q_ref[e] = image
                value = u_ref[e] - step * image
                u_ref[e] = value
                set_weights(e, value)

            pl.when(exists[e])(arrived)
        return rz, energy, beta, step

    one_row = zero_row + 1.0
    rz, energy, beta, step = lax.fori_loop(
        1, ITERS, iteration, (one_row, zero_row, zero_row, -one_row)
    )
    open_iteration(ITERS, beta, step, True)
    second_stage(ITERS)
    rz, energy, beta, step = scalars_of(ITERS, rz, energy)
    step_along(beta, step)
    for n, e in enumerate((1, 3)):
        resid_ref[n] = jnp.zeros((edge, cols), F32)

        def arrived(n=n, e=e):
            edge_arrival(ITERS, e).wait_recv()
            image = send[ITERS, e] - recv[ITERS, e] + dot(bt[rows(e)], z_ref[...])
            resid_ref[n] = r_ref[e] - step * (image + beta * s_ref[e])

        pl.when(exists[e])(arrived)

    for e in range(4):

        def sent(e=e):
            couple_copy(e).wait_send()
            image_copy(e).wait_send()

        pl.when(exists[e])(sent)

    @pl.loop(0, 2 * ITERS + 1)
    def _(t):
        for e in range(4):
            if e in (0, 2):
                pl.when(exists[e])(lambda e=e: edge_copy(t, e).wait_send())
            else:
                pl.when(exists[e] & (t != ITERS))(lambda e=e: edge_copy(t, e).wait_send())

    @pl.loop(0, ITERS + 1)
    def _(k):
        @pl.when(j > 0)
        def _():
            bytes_of(first.at[k, pl.ds(0, 2 * nx - 1)], f_send.at[k]).wait()

        @pl.when(j == 0)
        def _():
            bytes_of(first.at[k, pl.ds(0, nx - 1)], f_send.at[k]).wait()

        bytes_of(second.at[k, pl.ds(0, ny - 1)], g_send.at[k]).wait()


def per_device(loads, flex, schur, couple, corner_perm, coarse_inverse):
    nx = lax.axis_size("sx")
    ny = lax.axis_size("sy")
    iface, cols = loads.shape[2:]
    edge = iface // 4
    nc = coarse_inverse.shape[0]
    ncp = -(-nc // 128) * 128
    group = -(-(nx - 1) // 8) * 8 + 8
    kdim = ny * group
    perm = corner_perm.reshape(nx - 1, ny - 1).T
    perm = jnp.pad(perm, ((0, 1), (0, group - (nx - 1))), constant_values=-1).reshape(1, kdim)
    steps = 2 * ITERS + 1
    rounds = ITERS + 1
    vmem = pl.BlockSpec(memory_space=pltpu.VMEM)
    hbm = pl.BlockSpec(memory_space=pl.ANY)
    dma = pltpu.SemaphoreType.DMA
    out = jax.ShapeDtypeStruct((2, edge, cols), F32)
    mult, resid = pl.pallas_call(
        functools.partial(kernel, nx, ny, edge, group),
        out_shape=(out, out),
        in_specs=[vmem, hbm, hbm, vmem, vmem, vmem],
        out_specs=(vmem, vmem),
        scratch_shapes=[
            pltpu.VMEM((iface, iface), F32),
            pltpu.VMEM((4, 2 * edge, iface), BF16),
            pltpu.VMEM((iface, iface), BF16),
            pltpu.VMEM((ncp, ncp), F32),
            pltpu.VMEM((2, kdim, kdim), BF16),
            pltpu.VMEM((2, ZROWS + 8, kdim), BF16),
            pltpu.VMEM((group, 2 * nx * 8), BF16),
            pltpu.VMEM((32, iface), BF16),
            pltpu.VMEM((4, 8, edge), F32),
            pltpu.VMEM((4, 8, edge), F32),
            pltpu.VMEM((ZROWS, iface), F32),
            pltpu.VMEM((iface, 3 * ZROWS), BF16),
            pltpu.VMEM((4, ZROWS, edge), F32),
            pltpu.VMEM((4, ZROWS, edge), F32),
            pltpu.VMEM((iface, 3 * ZROWS), BF16),
            pltpu.VMEM((steps, 4, edge, cols), F32),
            pltpu.VMEM((steps, 4, edge, cols), F32),
            pltpu.VMEM((rounds, 8, cols), F32),
            pltpu.VMEM((rounds, 8, cols), F32),
            pltpu.VMEM((rounds, 2 * nx, 8, cols), F32),
            pltpu.VMEM((rounds, group, cols), F32),
            pltpu.VMEM((rounds, ny, group, cols), F32),
            pltpu.VMEM((4, edge, cols), F32),
            pltpu.VMEM((iface, 2 * cols), BF16),
            pltpu.VMEM((3 * ZROWS, cols), BF16),
            pltpu.VMEM((4, edge, cols), F32),
            pltpu.VMEM((4, edge, cols), F32),
            pltpu.VMEM((4, edge, cols), F32),
            pltpu.VMEM((2, edge, cols), F32),
            dma((4,)),
            dma,
            dma((4,)),
            dma((4,)),
            dma((4,)),
            dma((4,)),
            dma((steps, 4)),
            dma((steps, 4)),
            dma((rounds,)),
            dma((rounds,)),
            dma((rounds,)),
            dma((rounds,)),
        ],
        compiler_params=pltpu.CompilerParams(
            collective_id=0, has_side_effects=True, vmem_limit_bytes=48 * 1024 * 1024
        ),
    )(loads[0, 0], flex[0, 0], schur[0, 0], couple[0, 0], perm, coarse_inverse)
    return mult[None, None], resid[None, None]


def solution(mesh):
    placed = (
        P("sx", "sy", None, None),
        P("sx", "sy", None, None),
        P("sx", "sy", None, None),
        P("sx", "sy", None, None),
        P(),
        P(),
    )
    return jax.shard_map(
        per_device,
        mesh=mesh,
        in_specs=placed,
        out_specs=(P("sx", "sy", None, None, None), P("sx", "sy", None, None, None)),
        check_vma=False,
    )
```

time: 138 us -> 131 us (0.949)
  Pallas kernels: 130 us -> 123 us
    pallas_call x1, Pallas kernels: 130 us -> 123 us  [per_device(): pl.pallas_call(functools.partial(kernel, nx, ny, edge, group), out_shape=...]
where the time goes in v2:
time: 131 us
  Pallas kernels  123 us (94%)
  local copies, waits for them, and re-layouts  6.56 us (5%)
    pallas_call x1, Pallas kernels, per_device(): pl.pallas_call(functools.partial(kernel, nx, ny, edge, group), out_shape=...  123 us
    unnamed x11, local copies, waits for them, and re-layouts  5.7 us

profile of v2, /device:TPU:1, one launch (start us, length us, event | category | flops | bytes accessed | tf_op | source)
XLA Modules:
  0.0 130.6 jit_solution(12564461163922853351)
XLA Ops:
  0.6 0.8 reshape.10
  1.4 0.1 copy.9
  1.5 0.1 reshape.11.perm_ref
  1.6 0.0 copy-start
  1.6 1.6 %copy-done = bf16[1,1,1024,1024]{3,2,1,0:T(8,128)(2,1)S(1)} copy-done((bf16[1,1,1024,1024]{3,2,1,0:T(8,128)(2,1)S(1)}, bf16[1,1,1024,1024]{3,2,1,0:T(8,128)(2,1)}, u32[]{:S(2)}) %copy-start) | copy-done | bytes 2097176
  3.2 0.0 copy-start.1
  3.2 0.9 copy-done.1
  4.1 0.0 copy-start.2
  4.1 0.9 copy-done.2
  5.1 0.0 copy-start.3
  5.1 0.7 copy-done.3
  5.8 123.4 %shard_map.77 = (f32[2,256,128]{2,1,0:T(8,128)S(1)}, f32[2,256,128]{2,1,0:T(8,128)S(1)}) custom-call(bf16[1024,128]{1,0:T(8,128)(2,1)S(1)} %bitcast.8, f32[1024,1024]{1,0:T(8,128)} %bitcast.12, bf16[1024,1024]{1,0:T(8,128)(2,1)S(1)} %bitcast.7, f32[4,1024]{1,0:T(4,128)S(1)} %bitcast.11, s32[1,384]{1,0:T(1,128)S(1)} %reshape.11.perm_ref, f32[225,225]{1,0:T(8,128)S(1)} %copy-done.2), custom_call_target="tpu_custom_call" | custom-call | tf_op jit(solution)/shard_map/pallas_call | solution.py:477
  129.2 0.7 copy.12
  129.9 0.7 copy.13
  (1 shorter events, 0.0 us)
Async XLA Ops:
  1.6 1.6 %copy-start = (bf16[1,1,1024,1024]{3,2,1,0:T(8,128)(2,1)S(1)}, bf16[1,1,1024,1024]{3,2,1,0:T(8,128)(2,1)}, u32[]{:S(2)}) copy-start(bf16[1,1,1024,1024]{3,2,1,0:T(8,128)(2,1)} %param.8) | copy-start | bytes 6291460
  3.2 0.9 copy-start.1
  4.1 0.9 copy-start.2
  5.1 0.7 copy-start.3

commit v3 on v2

--- a/solution.py
+++ b/solution.py
@@ -39,13 +39,13 @@
 
 def kernel(
     nx, ny, edge, group,
-    loads_ref, flex_hbm, schur_hbm, couple_ref, perm_ref, cinv_ref,
+    loads_hbm, flex_hbm, schur_hbm, couple_hbm, perm_ref, cinv_hbm,
     mult_ref, resid_ref,
-    flex_v, flex_2, schur_v, cpad, ck_2, solve_2,
+    loads_ref, couple_ref, cinv_ref, flex_v, flex_2, schur_v, cpad, ck_2, solve_2,
     pick, cpl_2, cown, cnear, b_rows, bt, g_rows, g_near, mbt,
     recv, send, own_a, own_b, first, own_c, second,
     u_ref, weights, z_ref, r_ref, s_ref, q_ref, p_ref,
-    flex_sem, schur_sem, cs_sem, cr_sem, gs_sem, gr_sem,
+    in_sem, flex_sem, schur_sem, cs_sem, cr_sem, gs_sem, gr_sem,
     ex_send, ex_recv, f_send, f_recv, g_send, g_recv,
 ):
     i = lax.axis_index("sx")
@@ -53,7 +53,7 @@
     exists = (i > 0, i < nx - 1, j > 0, j < ny - 1)
     near = tuple((i + di, j + dj) for di, dj in NEAR)
     kdim = ny * group
-    cols = loads_ref.shape[1]
+    cols = loads_hbm.shape[1]
     highest = lax.Precision.HIGHEST
 
     def rows(e):
@@ -62,29 +62,39 @@
     def flex_copy(e):
         return pltpu.make_async_copy(flex_hbm.at[rows(e)], flex_v.at[rows(e)], flex_sem.at[e])
 
+    inputs = tuple(
+        pltpu.make_async_copy(source, target, in_sem.at[n])
+        for n, (source, target) in enumerate(
+            ((couple_hbm, couple_ref), (loads_hbm, loads_ref), (cinv_hbm, cinv_ref))
+        )
+    )
     for e in range(4):
         flex_copy(e).start()
-    schur_copy = pltpu.make_async_copy(schur_hbm, schur_v, schur_sem)
-    schur_copy.start()
-
     barrier = pltpu.get_barrier_semaphore()
 
-    @pl.loop(1, nx)
+    @pl.loop(1, nx, unroll=True)
     def _(d):
         pl.semaphore_signal(barrier, inc=1, device_id=(lax.rem(i + d, nx), j), device_id_type=MESH)
 
     @pl.when(j < ny - 1)
     def _():
-        @pl.loop(0, nx)
+        @pl.loop(0, nx, unroll=True)
         def _(d):
             pl.semaphore_signal(barrier, inc=1, device_id=(d, j + 1), device_id_type=MESH)
 
-    @pl.loop(0, ny)
+    @pl.loop(0, ny, unroll=True)
     def _(d):
         @pl.when((d != j) & (d != j + 1))
         def _():
             pl.semaphore_signal(barrier, inc=1, device_id=(i, d), device_id_type=MESH)
 
+    inputs[0].start()
+    inputs[1].start()
+    inputs[2].start()
+    schur_copy = pltpu.make_async_copy(schur_hbm, schur_v, schur_sem)
+    schur_copy.start()
+
+    inputs[0].wait()
     couple_all = couple_ref[...]
     zero6 = jnp.zeros((6, couple_all.shape[1]), F32)
     stacked = jnp.concatenate(
@@ -113,10 +123,18 @@
         first[:, nx:, :, :] = jnp.zeros((ITERS + 1, nx, 8, cols), F32)
 
     def coarse_operator():
+        inputs[2].wait()
         nc = cinv_ref.shape[0]
         cpad[...] = jnp.zeros_like(cpad)
         cpad[0:nc, 0:nc] = cinv_ref[...]
-        order = jnp.where(iota((cpad.shape[0], kdim), 0) == perm_ref[...], 1.0, 0.0).astype(BF16)
+        ncp = cpad.shape[0]
+        numbered = jnp.where(iota((ncp, nc), 0) == perm_ref[...], 1.0, 0.0).astype(BF16)
+        place = iota((nc, kdim), 1)
+        place_q = (place * (65536 // group + 1)) >> 16
+        place_p = place - group * place_q
+        lies = (place_p < nx - 1) & (place_q < ny - 1)
+        lies = lies & (iota((nc, kdim), 0) == place_p * (ny - 1) + place_q)
+        order = dot(numbered, jnp.where(lies, 1.0, 0.0).astype(BF16)).astype(BF16)
         m_id = iota((ZROWS + 8, kdim), 0)
         col = iota((ZROWS + 8, kdim), 1)
         block_row = (m_id * 43) >> 8
@@ -188,14 +206,17 @@
         product = product[0:16] + product[16:32]
         return product[:, :cols] + product[:, cols:]
 
-    def flex_products(k, e, last=False):
+    def flex_products(k, e):
         product = dot(flex_2[e], weights[...])
         product = product[:edge] + product[edge:]
         product = product[:, :cols] + product[:, cols:]
         send[k, e] = product
-        if e in (0, 2) or not last:
-            pl.when(exists[e])(lambda: edge_copy(k, e).start())
         return colsum(u_ref[e] * product)
+
+    def send_edges(k, last=False):
+        for e in range(4):
+            if e in (0, 2) or not last:
+                pl.when(exists[e])(lambda e=e: edge_copy(k, e).start())
 
     def schur_products(t):
         for e in range(4):
@@ -212,22 +233,25 @@
         own_b[k] = partial[8:16]
         first[k, i] = message
 
-        @pl.loop(1, nx)
-        def _(d):
-            pltpu.make_async_remote_copy(
-                src_ref=own_a.at[k], dst_ref=first.at[k, i],
-                send_sem=f_send.at[k], recv_sem=f_recv.at[k],
-                device_id=(lax.rem(i + d, nx), j), device_id_type=MESH,
-            ).start()
-
-        @pl.when(j > 0)
-        def _():
-            @pl.loop(0, nx)
-            def _(d):
+        @pl.loop(0, nx, unroll=True)
+        def _(n):
+            d = lax.rem(n + 1 + nx // 4, nx)
+            to = lax.rem(i + d, nx)
+
+            @pl.when(j > 0)
+            def _():
                 pltpu.make_async_remote_copy(
                     src_ref=own_b.at[k], dst_ref=first.at[k, nx + i],
                     send_sem=f_send.at[k], recv_sem=f_recv.at[k],
-                    device_id=(lax.rem(i + d, nx), j - 1), device_id_type=MESH,
+                    device_id=(to, j - 1), device_id_type=MESH,
+                ).start()
+
+            @pl.when(d != 0)
+            def _():
+                pltpu.make_async_remote_copy(
+                    src_ref=own_a.at[k], dst_ref=first.at[k, i],
+                    send_sem=f_send.at[k], recv_sem=f_recv.at[k],
+                    device_id=(to, j), device_id_type=MESH,
                 ).start()
 
     def second_stage(k):
@@ -244,8 +268,9 @@
         own_c[k] = summed
         second[k, j] = summed
 
-        @pl.loop(1, ny)
-        def _(d):
+        @pl.loop(0, ny - 1, unroll=True)
+        def _(n):
+            d = 1 + lax.rem(n + ny // 4, ny - 1)
             pltpu.make_async_remote_copy(
                 src_ref=own_c.at[k], dst_ref=second.at[k, j],
                 send_sem=g_send.at[k], recv_sem=g_recv.at[k],
@@ -289,11 +314,36 @@
             pl.when(exists[e])(arrived)
         schur_products(t)
 
+    def update_residual(k, beta, step):
+        for e in range(4):
+
+            def update(e=e):
+                image = send[k, e] - recv[k, e] + dot(bt[rows(e)], z_ref[...])
+                image = image + beta * s_ref[e]
+                s_ref[e] = image
+                r_ref[e] = r_ref[e] - step * image
+
+            pl.when(exists[e])(update)
+
+    def open_iteration(k, last):
+        flex_part = sum(flex_products(k, e) for e in range(4))
+        rz_part = 0.5 * sum(colsum(r_ref[e] * u_ref[e]) for e in range(4))
+        cross_part = 0.5 * sum(colsum(s_ref[e] * u_ref[e]) for e in range(4))
+        first_stage(k, corner_partials(), (rz_part, cross_part, flex_part))
+        send_edges(k, last)
+
+    inputs[1].wait()
     loads = loads_ref[...]
     weights[:, 0:cols] = loads
     weights[:, cols:] = jnp.zeros_like(loads)
     zero_row = jnp.zeros((1, cols), F32)
 
+    for e in range(4):
+        flex_copy(e).wait()
+        flex_2[e, 0:edge], flex_2[e, edge:] = halves(flex_v[rows(e)])
+        flex_products(0, e)
+    partial = corner_partials()
+
     sends_to = (nx - 1) + (ny - 1)
 
     @pl.when(j > 0)
@@ -304,13 +354,10 @@
     def _():
         pl.semaphore_wait(barrier, sends_to)
 
+    first_stage(0, partial, ())
     for e in range(4):
         pl.when(exists[e])(lambda e=e: couple_copy(e).start())
-    for e in range(4):
-        flex_copy(e).wait()
-        flex_2[e, 0:edge], flex_2[e, edge:] = halves(flex_v[rows(e)])
-        flex_products(0, e)
-    first_stage(0, corner_partials(), ())
+    send_edges(0)
 
     coarse_operator()
     for e in range(4):
@@ -334,7 +381,6 @@
         bt[rows(e)] = triple(b_rows[:, rows(e)])
 
     schur_copy.wait()
-    precondition_edges(0, ITERS + 1)
     b_high, b_low = halves(b_rows[...])
     contract1 = (((1,), (1,)), ((), ()))
     for e in range(4):
@@ -344,6 +390,7 @@
         )
         pl.when(exists[e])(lambda e=e: image_copy(e).start())
     second_stage(0)
+    precondition_edges(0, ITERS + 1)
     for e in range(4):
 
         def build(e=e):
@@ -355,6 +402,8 @@
 
         pl.when(exists[e])(build)
     coarse_solve(0, False)
+    one_row = zero_row + 1.0
+    update_residual(0, zero_row, -one_row)
     for e in range(4):
         weights[rows(e)] = jnp.zeros((edge, 2 * cols), BF16)
 
@@ -366,21 +415,6 @@
 
         pl.when(exists[e])(arrived)
 
-    def open_iteration(k, beta, step, last):
-        flex_part = sum(flex_products(k, e, last) for e in range(4))
-        for e in range(4):
-
-            def update(e=e):
-                image = send[k - 1, e] - recv[k - 1, e] + dot(bt[rows(e)], z_ref[...])
-                image = image + beta * s_ref[e]
-                s_ref[e] = image
-                r_ref[e] = r_ref[e] - step * image
-
-            pl.when(exists[e])(update)
-        rz_part = 0.5 * sum(colsum(r_ref[e] * u_ref[e]) for e in range(4))
-        cross_part = 0.5 * sum(colsum(s_ref[e] * u_ref[e]) for e in range(4))
-        first_stage(k, corner_partials(), (rz_part, cross_part, flex_part))
-
     def step_along(beta, step):
         for n, e in enumerate((1, 3)):
             direction = u_ref[e] + beta * p_ref[n]
@@ -388,13 +422,13 @@
             mult_ref[n] = mult_ref[n] + step * direction
 
     def iteration(k, carry):
-        rz, energy, beta, step = carry
         t = ITERS + 1 + k
-        open_iteration(k, beta, step, False)
+        open_iteration(k, False)
+        second_stage(k)
         precondition_edges(k, t)
-        second_stage(k)
-        rz, energy, beta, step = scalars_of(k, rz, energy)
+        rz, energy, beta, step = scalars_of(k, *carry)
         step_along(beta, step)
+        update_residual(k, beta, step)
         for e in range(4):
             weights[rows(e)] = jnp.zeros((edge, 2 * cols), BF16)
 
@@ -408,13 +442,10 @@
                 set_weights(e, value)
 
             pl.when(exists[e])(arrived)
-        return rz, energy, beta, step
-
-    one_row = zero_row + 1.0
-    rz, energy, beta, step = lax.fori_loop(
-        1, ITERS, iteration, (one_row, zero_row, zero_row, -one_row)
-    )
-    open_iteration(ITERS, beta, step, True)
+        return rz, energy
+
+    rz, energy = lax.fori_loop(1, ITERS, iteration, (one_row, zero_row))
+    open_iteration(ITERS, True)
     second_stage(ITERS)
     rz, energy, beta, step = scalars_of(ITERS, rz, energy)
     step_along(beta, step)
@@ -466,8 +497,6 @@
     ncp = -(-nc // 128) * 128
     group = -(-(nx - 1) // 8) * 8 + 8
     kdim = ny * group
-    perm = corner_perm.reshape(nx - 1, ny - 1).T
-    perm = jnp.pad(perm, ((0, 1), (0, group - (nx - 1))), constant_values=-1).reshape(1, kdim)
     steps = 2 * ITERS + 1
     rounds = ITERS + 1
     vmem = pl.BlockSpec(memory_space=pltpu.VMEM)
@@ -477,9 +506,12 @@
     mult, resid = pl.pallas_call(
         functools.partial(kernel, nx, ny, edge, group),
         out_shape=(out, out),
-        in_specs=[vmem, hbm, hbm, vmem, vmem, vmem],
+        in_specs=[hbm, hbm, hbm, hbm, vmem, hbm],
         out_specs=(vmem, vmem),
         scratch_shapes=[
+            pltpu.VMEM((iface, cols), BF16),
+            pltpu.VMEM((4, iface), F32),
+            pltpu.VMEM((nc, nc), F32),
             pltpu.VMEM((iface, iface), F32),
             pltpu.VMEM((4, 2 * edge, iface), BF16),
             pltpu.VMEM((iface, iface), BF16),
@@ -509,6 +541,7 @@
             pltpu.VMEM((4, edge, cols), F32),
             pltpu.VMEM((4, edge, cols), F32),
             pltpu.VMEM((2, edge, cols), F32),
+            dma((3,)),
             dma((4,)),
             dma,
             dma((4,)),
@@ -523,9 +556,9 @@
             dma((rounds,)),
         ],
         compiler_params=pltpu.CompilerParams(
-            collective_id=0, has_side_effects=True, vmem_limit_bytes=48 * 1024 * 1024
+            collective_id=0, has_side_effects=True, vmem_limit_bytes=60 * 1024 * 1024
         ),
-    )(loads[0, 0], flex[0, 0], schur[0, 0], couple[0, 0], perm, coarse_inverse)
+    )(loads[0, 0], flex[0, 0], schur[0, 0], couple[0, 0], corner_perm.reshape(1, nc), coarse_inverse)
     return mult[None, None], resid[None, None]
 
 

time: 131 us -> 119 us (0.908)
  Pallas kernels: 123 us -> 115 us
  local copies, waits for them, and re-layouts: 6.56 us -> 3.34 us
    pallas_call x1, Pallas kernels: 123 us -> 115 us  [per_device(): pl.pallas_call(functools.partial(kernel, nx, ny, edge, group), out_shape=...]
    unnamed x11 -> x2, local copies, waits for them, and re-layouts: 5.7 us -> 3.34 us
where the time goes in v3:
time: 119 us
  Pallas kernels  115 us (97%)
  local copies, waits for them, and re-layouts  3.34 us (3%)
    pallas_call x1, Pallas kernels, per_device(): pl.pallas_call(functools.partial(kernel, nx, ny, edge, group), out_shape=...  115 us
    unnamed x2, local copies, waits for them, and re-layouts  3.34 us

profile of v3, /device:TPU:1, one launch (start us, length us, event | category | flops | bytes accessed | tf_op | source)
XLA Modules:
  0.0 119.3 jit_solution(324161013525591623)
XLA Ops:
  0.6 115.3 %shard_map.77 = (f32[2,256,128]{2,1,0:T(8,128)}, f32[2,256,128]{2,1,0:T(8,128)}) custom-call(bf16[1024,128]{1,0:T(8,128)(2,1)} %bitcast.9, f32[1024,1024]{1,0:T(8,128)} %bitcast.7, bf16[1024,1024]{1,0:T(8,128)(2,1)} %bitcast.8, f32[4,1024]{1,0:T(4,128)} %bitcast.12, s32[1,225]{1,0:T(1,128)} %bitcast.13, f32[225,225]{1,0:T(8,128)} %cinv_hbm.1), custom_call_target="tpu_custom_call" | custom-call | tf_op jit(solution)/shard_map/pallas_call | solution.py:506
  115.9 1.7 %copy.10 = f32[1,1,2,256,128]{4,3,2,1,0:T(8,128)} copy(f32[1,1,2,256,128]{4,3,2,1,0:T(8,128)} %bitcast.11) | data formatting | bytes 524288
  117.6 1.7 %copy.11 = f32[1,1,2,256,128]{4,3,2,1,0:T(8,128)} copy(f32[1,1,2,256,128]{4,3,2,1,0:T(8,128)} %bitcast.10) | data formatting | bytes 524288

commit v4 on v3

--- a/solution.py
+++ b/solution.py
@@ -207,9 +207,8 @@
         return product[:, :cols] + product[:, cols:]
 
     def flex_products(k, e):
-        product = dot(flex_2[e], weights[...])
+        product = dot(flex_2[e], weights[:, 0:cols])
         product = product[:edge] + product[edge:]
-        product = product[:, :cols] + product[:, cols:]
         send[k, e] = product
         return colsum(u_ref[e] * product)
 
@@ -381,13 +380,13 @@
         bt[rows(e)] = triple(b_rows[:, rows(e)])
 
     schur_copy.wait()
-    b_high, b_low = halves(b_rows[...])
+    b_both = jnp.concatenate(halves(b_rows[...]), 0)
     contract1 = (((1,), (1,)), ((), ()))
     for e in range(4):
-        g_rows[e] = 0.25 * (
-            lax.dot_general(b_high, schur_v[rows(e)], contract1, preferred_element_type=F32)
-            + lax.dot_general(b_low, schur_v[rows(e)], contract1, preferred_element_type=F32)
-        )
+        product = lax.dot_general(
+            b_both, schur_v[rows(e)], contract1, preferred_element_type=F32
+        )
+        g_rows[e] = 0.25 * (product[:ZROWS] + product[ZROWS:])
         pl.when(exists[e])(lambda e=e: image_copy(e).start())
     second_stage(0)
     precondition_edges(0, ITERS + 1)
@@ -414,6 +413,21 @@
             set_weights(e, value)
 
         pl.when(exists[e])(arrived)
+
+    def edges_sent(t, which=range(4)):
+        for e in which:
+            pl.when(exists[e])(lambda e=e: edge_copy(t, e).wait_send())
+
+    def sums_sent(k):
+        @pl.when(j > 0)
+        def _():
+            bytes_of(first.at[k, pl.ds(0, 2 * nx - 1)], f_send.at[k]).wait()
+
+        @pl.when(j == 0)
+        def _():
+            bytes_of(first.at[k, pl.ds(0, nx - 1)], f_send.at[k]).wait()
+
+        bytes_of(second.at[k, pl.ds(0, ny - 1)], g_send.at[k]).wait()
 
     def step_along(beta, step):
         for n, e in enumerate((1, 3)):
@@ -467,25 +481,15 @@
 
         pl.when(exists[e])(sent)
 
+    edges_sent(ITERS, (0, 2))
+
     @pl.loop(0, 2 * ITERS + 1)
     def _(t):
-        for e in range(4):
-            if e in (0, 2):
-                pl.when(exists[e])(lambda e=e: edge_copy(t, e).wait_send())
-            else:
-                pl.when(exists[e] & (t != ITERS))(lambda e=e: edge_copy(t, e).wait_send())
+        pl.when(t != ITERS)(lambda: edges_sent(t))
 
     @pl.loop(0, ITERS + 1)
     def _(k):
-        @pl.when(j > 0)
-        def _():
-            bytes_of(first.at[k, pl.ds(0, 2 * nx - 1)], f_send.at[k]).wait()
-
-        @pl.when(j == 0)
-        def _():
-            bytes_of(first.at[k, pl.ds(0, nx - 1)], f_send.at[k]).wait()
-
-        bytes_of(second.at[k, pl.ds(0, ny - 1)], g_send.at[k]).wait()
+        sums_sent(k)
 
 
 def per_device(loads, flex, schur, couple, corner_perm, coarse_inverse):

time: 119 us -> 120 us (level)
  no operation moved by 1% of the time
where the time goes in v4:
time: 120 us
  Pallas kernels  116 us (97%)
  local copies, waits for them, and re-layouts  3.34 us (3%)
    pallas_call x1, Pallas kernels, per_device(): pl.pallas_call(functools.partial(kernel, nx, ny, edge, group), out_shape=...  116 us
    unnamed x2, local copies, waits for them, and re-layouts  3.34 us

profile of v4, /device:TPU:1, one launch (start us, length us, event | category | flops | bytes accessed | tf_op | source)
XLA Modules:
  0.0 119.6 jit_solution(9220423011786284736)
XLA Ops:
  0.6 115.6 %shard_map.77 = (f32[2,256,128]{2,1,0:T(8,128)}, f32[2,256,128]{2,1,0:T(8,128)}) custom-call(bf16[1024,128]{1,0:T(8,128)(2,1)} %bitcast.9, f32[1024,1024]{1,0:T(8,128)} %bitcast.7, bf16[1024,1024]{1,0:T(8,128)(2,1)} %bitcast.8, f32[4,1024]{1,0:T(4,128)} %bitcast.12, s32[1,225]{1,0:T(1,128)} %bitcast.13, f32[225,225]{1,0:T(8,128)} %cinv_hbm.1), custom_call_target="tpu_custom_call" | custom-call | tf_op jit(solution)/shard_map/pallas_call | solution.py:510
  116.2 1.7 %copy.10 = f32[1,1,2,256,128]{4,3,2,1,0:T(8,128)} copy(f32[1,1,2,256,128]{4,3,2,1,0:T(8,128)} %bitcast.11) | data formatting | bytes 524288
  117.9 1.7 %copy.11 = f32[1,1,2,256,128]{4,3,2,1,0:T(8,128)} copy(f32[1,1,2,256,128]{4,3,2,1,0:T(8,128)} %bitcast.10) | data formatting | bytes 524288
